TPU v7x, 128 devices: a whole 4x4x4 slice. The times are simulated.
128 devices in a mesh: shard: 128 (over x, y, z, core).
Axes of the slice: x: 4, y: 4, z: 4, core: 2. Of those that a mesh axis runs over, the one named last changes fastest.
Arguments:
- embeddings: bfloat16 [262144, 1024], P('shard'), may hold values from -6 to 6
- block_rows: int32 [2048], P('shard'), may hold values from 1 to 128, 196608 in all
- pairs: int32 [65536, 3], P('shard'), may hold values from 0 to 2047, as said below
Outputs:
- best: float32 [2048, 128], P('shard')
Inputs may be any that keep to these rules, and one draw needn't show every extreme that they name: `pairs`: entries d * 512 to (d + 1) * 512 - 1 are device d's. Each is (row block, column block, scorer); the scorer is d for a live entry and 128 for an unused one. The column block is always one of device d's blocks; the row block is one of device d's or of another device. Exactly 64 entries of device d have a row block of another device, all live, each from a different device; and the blocks of each device are row blocks of such entries of exactly 64 other devices. Live entries of one device number 64 to 512, and some device has 512.
All inputs are finite; a program needn't handle non-finite values. No bound on the sum of `block_rows` on one device may be relied on, other than what follows from the above.
Results may differ from a plain program's by a relative error of at most 0.0003.
Values may be sent and summed in bfloat16 or wider, within the bound.
No kernel may reach another device: no remote copies, remote signals or barrier semaphores. Data moves between devices by JAX's collectives and lax.ppermute only.
A program may use at most 256 MiB of HBM per device.

v0:
```python
import functools

import jax
import jax.numpy as jnp
import numpy as np
from jax import lax
from jax.experimental import pallas as pl
from jax.experimental.pallas import tpu as pltpu
from jax.sharding import PartitionSpec as P

UNIT = 16
CLASSES = 4
COLORS = 2 * CLASSES
LOG_COLORS = 3
PLANS = ((7, 16, 24), (8, 16, 16), (16, 0, 0))
SHARE = 8
MIB = 1024 * 1024


def turns(direct):
    return -(-(2 * 16 - 2 * direct) // COLORS)


def ask_kernel(me_ref, pairs_ref, rows_ref, tell_ref):
    device = me_ref[0]
    peers, _, columns = tell_ref.shape
    row, col = pairs_ref[0:1, :], pairs_ref[1:2, :]
    owner = row >> 4
    far = (pairs_ref[2:3, :] == device) & (owner != device)
    peer = lax.broadcasted_iota(jnp.int32, (peers, row.shape[1]), 0)
    code = (row & 15) * 16 + (col & 15)
    code = jnp.where((owner == peer) & far, code, -1).astype(jnp.float32)
    most = code[:, :peers]
    for k in range(1, row.shape[1] // peers):
        most = jnp.maximum(most, code[:, k * peers : (k + 1) * peers])
    wanted = jnp.max(most.T, axis=0, keepdims=True).astype(jnp.int32)
    tell = jnp.concatenate([wanted, rows_ref[...]], axis=1)
    tell_ref[...] = jnp.broadcast_to(tell[None], tell_ref.shape)


def ask(device, pairs, block_rows, peers):
    blocks = block_rows.shape[0]
    assert blocks == 16
    vmem = pl.BlockSpec(memory_space=pltpu.VMEM)
    return pl.pallas_call(
        ask_kernel,
        in_specs=[pl.BlockSpec(memory_space=pltpu.SMEM), vmem, vmem],
        out_specs=vmem,
        out_shape=jax.ShapeDtypeStruct((peers, 1, peers + blocks), jnp.int32),
        name="ask",
    )(device.reshape(1), pairs.T, block_rows.reshape(1, blocks))


def normalize_kernel(after_ref, values_ref, unit_ref):
    values = values_ref[...].astype(jnp.float32)
    total = jnp.sum(values * values, axis=-1, keepdims=True)
    unit_ref[...] = (values * lax.rsqrt(total + 1e-06)).astype(jnp.bfloat16)


def normalize(embeddings, after):
    rows, depth = embeddings.shape
    step = 1024
    return pl.pallas_call(
        normalize_kernel,
        grid=(rows // step,),
        in_specs=[pl.BlockSpec(memory_space=pl.ANY), pl.BlockSpec((step, depth), lambda i: (i, 0))],
        out_specs=pl.BlockSpec((step, depth), lambda i: (i, 0)),
        out_shape=jax.ShapeDtypeStruct((rows, depth), jnp.bfloat16),
        cost_estimate=pl.CostEstimate(flops=4 * rows * depth, bytes_accessed=4 * rows * depth, transcendentals=rows),
        name="normalize",
    )(after, embeddings)


def near_pairs(blocks):
    return np.array([(i, j) for i in range(blocks // 4) for j in range(blocks // 2) if (j + 1) * 2 > i * 4], np.int32)


def score_near(near, linked, counts, rows_ref, best_ref, kept):
    blocks, width, depth = rows_ref.shape[0] // 2, rows_ref.shape[1], rows_ref.shape[2]
    kept[...] = jnp.full(kept.shape, -1.0, jnp.float32)
    i = lax.broadcasted_iota(jnp.int32, (width, width), 0)
    j = lax.broadcasted_iota(jnp.int32, (width, width), 1)

    def step(number, carry):
        left, right = near[2 * number], near[2 * number + 1]
        rows = rows_ref[pl.ds(left * 4, 4)].reshape(4 * width, depth)
        cols = rows_ref[pl.ds(right * 2, 2)].reshape(2 * width, depth)
        scores = lax.dot_general(rows, cols, (((1,), (1,)), ((), ())), preferred_element_type=jnp.float32)
        for b in range(2):
            c = right * 2 + b
            most = best_ref[pl.ds(c, 1), :]
            for a in range(4):
                r = left * 4 + a
                limit = jnp.where(linked[r * blocks + c] > 0, counts[r], 0)
                keep = (i < limit) & (j < counts[c]) & ((r != c) | (i != j))
                part = jnp.where(keep, scores[a * width : (a + 1) * width, b * width : (b + 1) * width], -1.0)
                kept[r] = jnp.maximum(kept[r], part)
                most = jnp.maximum(most, jnp.max(part, axis=0, keepdims=True))
            best_ref[pl.ds(c, 1), :] = most
        return carry

    lax.fori_loop(0, len(near_pairs(blocks)), step, 0)
    for b in range(blocks):
        best_ref[pl.ds(b, 1), :] = jnp.maximum(best_ref[pl.ds(b, 1), :], jnp.max(kept[b].T, axis=0, keepdims=True))


def exact_dot(a, b):
    return jnp.dot(
        a.astype(jnp.float32).astype(jnp.bfloat16),
        b.astype(jnp.float32).astype(jnp.bfloat16),
        preferred_element_type=jnp.float32,
    ).astype(jnp.int32)


def flip(a):
    return a.astype(jnp.float32).T.astype(jnp.int32)


def plan_kernel(
    direct, items, relayed, chips, me_ref, pair_ref, count_ref, count_t_ref,
    send_ref, far_ref, code_ref, far_code_ref, hand_ref, target_ref, back_ref, fits_ref,
    w_lo, w_hi, sums, mine,
):
    device = me_ref[0]
    chip, core = device // 2, device % 2
    devices = 2 * chips
    flat = (chips, chips)
    pair = pair_ref[...]
    code = jnp.maximum(pair, 0)
    row_of, col_of = code >> 4, code & 15
    row_count = jnp.zeros(pair.shape, jnp.int32)
    col_count = jnp.zeros(pair.shape, jnp.int32)
    for l in range(16):
        row_count = jnp.where(row_of == l, count_t_ref[pl.ds(l, 1), :], row_count)
        col_count = jnp.where(col_of == l, count_ref[:, l : l + 1], col_count)

    xs = lax.broadcasted_iota(jnp.int32, (chips, devices), 0)
    ds = lax.broadcasted_iota(jnp.int32, (chips, devices), 1)
    pick = [(ds == 2 * xs + i).astype(jnp.int32) for i in range(2)]
    pick_t = [flip(p) for p in pick]

    def split(values):
        half = [exact_dot(p, values) for p in pick]
        return [[exact_dot(half[i], pick_t[j]) for j in range(2)] for i in range(2)]

    asked = {"code": split(pair + 1), "row": split(row_count), "col": split(col_count)}
    asked_t = {k: [[flip(v[j][i]) for j in range(2)] for i in range(2)] for k, v in asked.items()}

    x = lax.broadcasted_iota(jnp.int32, flat, 0)
    y = lax.broadcasted_iota(jnp.int32, flat, 1)
    low, same = x <= y, x == y
    edges = []
    for kind in range(2):
        for p in range(2):
            for q in range(2):
                first, second = (asked_t, asked) if kind == 0 else (asked, asked_t)
                here = {k: jnp.where(low, first[k][p][q], second[k][q][p]) for k in asked}
                exists = here["code"] > 0
                if kind == 1:
                    exists = exists & ~same
                number = jnp.maximum(here["code"] - 1, 0)
                r, c = number >> 4, number & 15
                side = jnp.where(low, p, q) * 16
                other = jnp.where(low, q, p) * 16
                owns_row = low if kind == 0 else ~low
                own_block = side + jnp.where(owns_row, r, c)
                other_block = other + jnp.where(owns_row, c, r)
                own_rows = jnp.where(exists, jnp.where(owns_row, here["row"], here["col"]), 0)
                other_rows = jnp.where(exists, jnp.where(owns_row, here["col"], here["row"]), 0)
                edges.append((exists, own_block, other_block, own_rows, other_rows))
    for e, (exists, _, _, own_rows, other_rows) in enumerate(edges):
        own_units, other_units = (own_rows + 15) >> 4, (other_rows + 15) >> 4
        w_lo[e] = jnp.where(low, own_units, other_units)
        w_hi[e] = jnp.where(low, other_units, own_units)

    for half in range(2):
        for choice in range(16):
            up = jnp.zeros(flat, jnp.int32)
            down = jnp.zeros(flat, jnp.int32)
            for b in range(4):
                if choice >> b & 1:
                    up = up + w_lo[half * 4 + b]
                else:
                    down = down + w_hi[half * 4 + b]
            lanes = pl.ds(0, chips) if half or choice < 8 else pl.ds(chips, chips)
            spot = choice if half else choice % 8
            sums[half, spot, :, lanes] = up
            sums[2 + half, spot, :, lanes] = down
            if half:
                sums[1, spot, :, pl.ds(chips, chips)] = up
                sums[3, spot, :, pl.ds(chips, chips)] = down
    eight = jnp.where(lax.broadcasted_iota(jnp.int32, (chips, devices), 1) < chips, 0, 8)

    def try_half(a, least):
        up_a, down_a = sums[0, a] - 2 * direct, sums[2, a] - 2 * direct
        for b in range(16):
            up, down = up_a + sums[1, b], down_a + sums[3, b]
            over = jnp.maximum(up, 0) + jnp.maximum(down, 0)
            rank = over * 65536 + jnp.maximum(up, down) * 256 + (b * 16 + a) + eight
            least = jnp.minimum(least, rank)
        return least

    least = lax.fori_loop(0, 8, try_half, jnp.full((chips, devices), 2**30, jnp.int32))
    least = jnp.minimum(least[:, :chips], least[:, chips:])
    chosen = jnp.where(same, 255, least & 255)

    out_total = jnp.zeros(flat, jnp.int32)
    in_total = jnp.zeros(flat, jnp.int32)
    for e, (exists, own_block, other_block, own_rows, other_rows) in enumerate(edges):
        bit = (chosen >> e) & 1
        sends = exists & ((bit == 1) == low)
        out_units = jnp.where(sends, (own_rows + 15) >> 4, 0)
        in_rows = jnp.where(same, own_rows, other_rows)
        in_units = jnp.where((exists & ~sends) | same, (in_rows + 15) >> 4, 0)
        out_total = out_total + out_units
        in_total = in_total + in_units
        mine[e] = out_units
        mine[8 + e] = own_block ^ (core * 16)
        mine[16 + e] = in_units
        mine[24 + e] = jnp.where(same, other_block, own_block) ^ (core * 16)
        mine[32 + e] = in_rows
    mine[40] = out_total
    mine[41] = in_total

    far = jnp.maximum(out_total - 2 * direct, 0)
    before = exact_dot(far, (x < y).astype(jnp.int32))
    total = jnp.sum(far, axis=1, keepdims=True)
    at_self = jnp.sum(jnp.where(same, before, 0), axis=1, keepdims=True)
    rank = before - at_self + jnp.where(y < x, total, 0)
    over_out = jnp.max((total + COLORS - 1) >> LOG_COLORS)
    over_in = jnp.zeros((), jnp.int32)
    earlier = (y < x).astype(jnp.int32)
    number, place, first = [], [], []
    for color in range(COLORS):
        first.append((color - rank) & (COLORS - 1))
        number.append((far - first[-1] + COLORS - 1) >> LOG_COLORS)
        over_in = jnp.maximum(over_in, jnp.max(jnp.sum(number[-1], axis=0, keepdims=True)))
        place.append(exact_dot(earlier, number[-1]))
    room = turns(direct)
    fits = (over_out <= items) & (over_in <= relayed) & (jnp.max(far) <= room * COLORS)
    fits_ref[0] = fits.astype(jnp.int32)
    odd = core == 1
    own_class = chip // (chips // CLASSES)
    hand_number = jnp.zeros(flat, jnp.int32)
    hand_place = jnp.zeros(flat, jnp.int32)
    hand_first = jnp.zeros(flat, jnp.int32)
    for k in range(CLASSES):
        picked = [jnp.where(odd, v[2 * k + 1], v[2 * k]) for v in (number, place, first)]
        for n, v in enumerate(picked):
            mine[47 + 6 * k + n] = flip(v)
        here = own_class == k
        hand_number = jnp.where(here, picked[0], hand_number)
        hand_place = jnp.where(here, picked[1], hand_place)
        hand_first = jnp.where(here, picked[2], hand_first)
    mine[42] = rank
    mine[43] = far
    own = pl.ds(chip, 1)

    out_units = [mine[e, own, :] for e in range(SHARE)]
    out_block = [mine[8 + e, own, :] for e in range(SHARE)]
    in_units = [mine[16 + e, own, :] for e in range(SHARE)]
    in_block = [mine[24 + e, own, :] for e in range(SHARE)]
    in_rows = [mine[32 + e, own, :] for e in range(SHARE)]
    out_total, in_total, rank_own, far_own = (mine[40 + k, own, :] for k in range(4))

    def lane(total):
        plain = jnp.minimum(total, 2 * direct)
        half = (plain + 1) >> 1
        return jnp.where(odd, half, 0), jnp.where(odd, plain - half, half)

    def unit_at(position, valid):
        value = jnp.full(position.shape, -1, jnp.int32)
        start = jnp.zeros((1, chips), jnp.int32)
        for e in range(SHARE):
            hit = valid & (position >= start) & (position < start + out_units[e])
            value = jnp.where(hit, out_block[e] * 8 + position - start, value)
            start = start + out_units[e]
        return value

    def code_at(position, valid):
        value = jnp.zeros(position.shape, jnp.int32)
        start = jnp.zeros((1, chips), jnp.int32)
        for e in range(SHARE):
            hit = valid & (position >= start) & (position < start + in_units[e])
            rows = jnp.minimum(in_rows[e] - UNIT * (position - start), UNIT)
            value = jnp.where(hit, in_block[e] * 32 + 32 + rows, value)
            start = start + in_units[e]
        return value

    step = lax.broadcasted_iota(jnp.int32, (direct, chips), 0)
    begin, length = lane(out_total)
    plain = unit_at(begin + step, step < length)
    send_ref[...] = jnp.maximum(plain, 0)
    target_ref[pl.ds(0, direct), :] = plain
    begin, length = lane(in_total)
    code_ref[...] = code_at(begin + step, step < length)

    if items:
        slot = lax.broadcasted_iota(jnp.int32, (items, chips), 0)
        place_in = lax.broadcasted_iota(jnp.int32, (relayed, chips), 0)
        for k in range(CLASSES):
            turn = COLORS * slot + 2 * k + core - rank_own
            unit = unit_at(2 * direct + turn, (turn >= 0) & (turn < far_own))
            far_ref[:, k : k + 1] = jnp.sum(jnp.maximum(unit, 0), axis=1, keepdims=True)
            number_t, place_t, first_t = (mine[47 + 6 * k + n, own, :] for n in range(3))
            made = jnp.zeros((relayed, chips), jnp.int32)
            for n in range(room):
                first = (2 * k + core - rank_own) & (COLORS - 1)
                target_ref[pl.ds(direct + CLASSES * n + k, 1), :] = unit_at(
                    2 * direct + first + COLORS * n, n < (far_own - first + COLORS - 1) >> LOG_COLORS
                )
                back_ref[pl.ds(CLASSES * n + k, 1), :] = jnp.where(n < number_t, place_t + n, -1)
                hit = (place_t + n == place_in) & (n < number_t)
                made = made + code_at(2 * direct + first_t + COLORS * n + 0 * place_in, hit)
            far_code_ref[:, k : k + 1] = jnp.sum(made, axis=1, keepdims=True)
        hand_number, hand_place, hand_from = (
            flip(hand_number), flip(hand_place), flip((rank + hand_first) >> LOG_COLORS)
        )
        for q in range(relayed):
            value = jnp.zeros(flat, jnp.int32)
            for n in range(room):
                hit = (hand_place + n == q) & (n < hand_number)
                value = value + jnp.where(hit, y * items + hand_from + n, 0)
            hand_ref[:, q : q + 1] = jnp.sum(value, axis=1, keepdims=True)


def make_plan(direct, items, relayed, told, device):
    devices, columns = told.shape
    chips = devices // 2
    ints = lambda *shape: jax.ShapeDtypeStruct(shape, jnp.int32)
    vmem = pl.BlockSpec(memory_space=pltpu.VMEM)
    return pl.pallas_call(
        functools.partial(plan_kernel, direct, items, relayed, chips),
        in_specs=[pl.BlockSpec(memory_space=pltpu.SMEM), vmem, vmem, vmem],
        out_specs=[vmem] * 7 + [pl.BlockSpec(memory_space=pltpu.SMEM)],
        out_shape=[
            ints(direct, chips),
            ints(max(items, 8), CLASSES),
            ints(direct, chips),
            ints(max(relayed, 8), CLASSES),
            ints(chips, max(relayed, 8)),
            ints(direct + turns(direct) * CLASSES, chips),
            ints(max(turns(direct), 1) * CLASSES, chips),
            ints(1),
        ],
        scratch_shapes=[
            pltpu.VMEM((SHARE, chips, chips), jnp.int32),
            pltpu.VMEM((SHARE, chips, chips), jnp.int32),
            pltpu.VMEM((4, 16, chips, devices), jnp.int32),
            pltpu.VMEM((44 + 6 * CLASSES, chips, chips), jnp.int32),
        ],
        compiler_params=pltpu.CompilerParams(vmem_limit_bytes=32 * MIB),
        cost_estimate=pl.CostEstimate(flops=10**11, bytes_accessed=10**6, transcendentals=0),
        name="plan",
    )(device.reshape(1), told[:, :devices], told[:, devices:], told[:, devices:].T)


def turn(first, second, values):
    rows = first * second
    o = lax.broadcasted_iota(jnp.int32, (rows, rows), 0)
    i = lax.broadcasted_iota(jnp.int32, (rows, rows), 1)
    take = ((o % first) * second + o // first == i).astype(jnp.float32).astype(jnp.bfloat16)
    return jnp.dot(take, values, preferred_element_type=jnp.float32).astype(jnp.bfloat16)


def fetch(near_ref, far_ref, held, sems):
    half = near_ref.shape[0]
    copies = [
        pltpu.make_async_copy(near_ref, held.at[pl.ds(0, half)], sems.at[0]),
        pltpu.make_async_copy(far_ref, held.at[pl.ds(half, half)], sems.at[1]),
    ]
    for copy in copies:
        copy.start()
    for copy in copies:
        copy.wait()


def pack_kernel(group, direct, items, send, far, near_ref, far_ref, out_ref, held, gathered, turned, sems):
    step = pl.program_id(0)
    chips = pl.num_programs(0) * group

    @pl.when(step == 0)
    def _():
        fetch(near_ref, far_ref, held, sems)
        if items:
            for p in range(CLASSES):
                for q in range(items):
                    gathered[pl.ds(q * UNIT, UNIT), :] = held[far[q * CLASSES + p]]
                size = items * UNIT
                turned[pl.ds(p * size, size), :] = turn(items, UNIT, gathered[...])

    for k in range(group):
        slot = step * group + k
        for p in range(direct):
            out_ref[k, pl.ds(p * UNIT, UNIT), :] = held[send[p * chips + slot]]
        if items:
            out_ref[k, pl.ds(direct * UNIT, items), :] = turned[pl.ds(pl.multiple_of(slot * items, items), items), :]


def pack(direct, items, send, far, near_units, far_units):
    units, _, depth = near_units.shape
    chips = send.shape[1]
    rows = direct * UNIT + items
    group = 8 if items else 4
    some = max(items, 16)
    return pl.pallas_call(
        functools.partial(pack_kernel, group, direct, items),
        grid_spec=pltpu.PrefetchScalarGridSpec(
            num_scalar_prefetch=2,
            grid=(chips // group,),
            in_specs=[pl.BlockSpec(memory_space=pl.ANY)] * 2,
            out_specs=pl.BlockSpec((group, rows, depth), lambda i, *_: (i, 0, 0)),
            scratch_shapes=[
                pltpu.VMEM((2 * units, UNIT, depth), jnp.bfloat16),
                pltpu.VMEM((some * UNIT, depth), jnp.bfloat16),
                pltpu.VMEM((some * chips, depth), jnp.bfloat16),
                pltpu.SemaphoreType.DMA((2,)),
            ],
        ),
        out_shape=jax.ShapeDtypeStruct((chips, rows, depth), jnp.bfloat16),
        compiler_params=pltpu.CompilerParams(vmem_limit_bytes=20 * MIB),
        name="pack",
    )(send.reshape(-1), far.reshape(-1), near_units, far_units)


def relay_kernel(hand_ref, held_ref, target_ref, back_ref, out_ref, target_out, back_out):
    target_out[...] = target_ref[...]
    back_out[...] = back_ref[...]
    held = held_ref[...]
    rows = held.shape[0] * held.shape[1]
    hand = hand_ref[...]
    slots, relayed = hand.shape
    o = lax.broadcasted_iota(jnp.int32, (slots * relayed, slots), 0)
    spread = (o // relayed == lax.broadcasted_iota(jnp.int32, o.shape, 1)).astype(jnp.int32)
    each = exact_dot(spread, hand >> 4) * 16 + exact_dot(spread, hand & 15)
    o = lax.broadcasted_iota(jnp.int32, each.shape, 0)
    own = o % relayed == lax.broadcasted_iota(jnp.int32, each.shape, 1)
    source = jnp.sum(jnp.where(own, each, 0), axis=1, keepdims=True)
    i = lax.broadcasted_iota(jnp.int32, (out_ref.shape[0], rows), 1)
    take = (source == i).astype(jnp.float32).astype(jnp.bfloat16)
    out_ref[...] = jnp.dot(
        take, held.reshape(rows, held.shape[2]), preferred_element_type=jnp.float32
    ).astype(jnp.bfloat16)


def relay(hand, arrived, target, back, direct, items):
    chips, relayed = hand.shape
    depth = arrived.shape[2]
    step = chips * relayed // 2
    tables = [pl.BlockSpec(t.shape, lambda i: (0, 0)) for t in (target, back)]
    passed, target, back = pl.pallas_call(
        relay_kernel,
        grid=(chips * relayed // step,),
        in_specs=[
            pl.BlockSpec((chips // 2, relayed), lambda i: (i, 0)),
            pl.BlockSpec((chips, items, depth), lambda i: (0, direct * UNIT // items, 0)),
            *tables,
        ],
        out_specs=[pl.BlockSpec((step, depth), lambda i: (i, 0)), *tables],
        out_shape=[
            jax.ShapeDtypeStruct((chips * relayed, depth), jnp.bfloat16),
            jax.ShapeDtypeStruct(target.shape, jnp.int32),
            jax.ShapeDtypeStruct(back.shape, jnp.int32),
        ],
        compiler_params=pltpu.CompilerParams(vmem_limit_bytes=54 * MIB),
        name="relay",
    )(hand, arrived, target, back)
    return passed.reshape(chips, relayed, depth), target, back


def score_kernel(
    places, group, turned, codes, counts, near, linked, near_ref, far_ref, arrived_ref, back_ref, best_ref,
    held, rows_held, batch, tiles, kept, head, follow, sems,
):
    slots = back_ref.shape[0]
    blocks, width, _ = held.shape
    copies = [
        pltpu.make_async_copy(near_ref, held.at[pl.ds(0, blocks // 2)], sems.at[0]),
        pltpu.make_async_copy(far_ref, held.at[pl.ds(blocks // 2, blocks // 2)], sems.at[1]),
    ]
    if turned:
        copies.insert(0, pltpu.make_async_copy(arrived_ref, rows_held, sems.at[2]))
    else:
        copies.append(pltpu.make_async_copy(arrived_ref.at[:, pl.ds(0, places * UNIT)], rows_held, sems.at[2]))
    for copy in copies:
        copy.start()
    best_ref[...] = jnp.full(best_ref.shape, -1.0, jnp.float32)
    tiles[...] = jnp.full(tiles.shape, -1.0, jnp.float32)

    def clear(b, carry):
        head[b] = -1
        return carry

    lax.fori_loop(0, blocks, clear, 0)

    def link(slot, carry):
        for p in range(places):
            made = codes[p * slots + slot]
            block = jnp.maximum((made >> 5) - 1, 0)
            unit = slot * 32 + p

            @pl.when(made > 0)
            def _():
                follow[unit] = head[block]
                head[block] = unit

        return carry

    lax.fori_loop(0, slots, link, 0)
    copies[0].wait()
    if turned:
        for slot in range(slots):
            rows_held[slot] = turn(UNIT, places, rows_held[slot])
    else:
        score_near(near, linked, counts, held, best_ref, kept)
    for copy in copies[1:]:
        copy.wait()

    i = lax.broadcasted_iota(jnp.int32, (UNIT, width), 0)
    j = lax.broadcasted_iota(jnp.int32, (UNIT, width), 1)

    def per_block(block, carry):
        columns = j < counts[block]

        def some_units(unit):
            taken = []
            for g in range(group):
                live = unit >= 0
                here = jnp.maximum(unit, 0)
                slot, p = here >> 5, here & 31
                batch[pl.ds(g * UNIT, UNIT), :] = rows_held[slot, pl.ds(pl.multiple_of(p * UNIT, UNIT), UNIT), :]
                rows = jnp.where(live, codes[p * slots + slot] & 31, 0)
                taken.append((jnp.where(live, slot, slots), p, rows))
                unit = jnp.where(live, follow[here], -1)
            scores = lax.dot_general(
                batch[...], held[block], (((1,), (1,)), ((), ())), preferred_element_type=jnp.float32
            )
            most = best_ref[pl.ds(block, 1), :]
            for g, (slot, p, rows) in enumerate(taken):
                tile = jnp.where((i < rows) & columns, scores[g * UNIT : (g + 1) * UNIT], -1.0)
                tiles[slot, pl.ds(pl.multiple_of(p * UNIT, UNIT), UNIT), :] = tile
                most = jnp.maximum(most, jnp.max(tile, axis=0, keepdims=True))
            best_ref[pl.ds(block, 1), :] = most
            return unit

        lax.while_loop(lambda unit: unit >= 0, some_units, head[block])
        return carry

    lax.fori_loop(0, blocks, per_block, 0)

    if slots % 8 == 0:

        def finish(part, carry):
            for k in range(8):
                slot = part * 8 + k
                back_ref[pl.ds(slot, 1), :] = jnp.max(tiles[slot].T, axis=0, keepdims=True)
            return carry

        lax.fori_loop(0, slots // 8, finish, 0)
    else:
        for slot in range(slots):
            back_ref[slot : slot + 1, :] = jnp.max(tiles[slot].T, axis=0, keepdims=True)


def score(codes, counts, linked, near, far, arrived, group, turned):
    blocks, width, depth = near.shape
    places, slots = codes.shape
    rows = places * UNIT
    any_place = pl.BlockSpec(memory_space=pl.ANY)
    vmem = pl.BlockSpec(memory_space=pltpu.VMEM)
    smem = pl.BlockSpec(memory_space=pltpu.SMEM)
    return pl.pallas_call(
        functools.partial(score_kernel, places, group, turned),
        in_specs=[smem, smem, smem, smem, any_place, any_place, any_place],
        out_specs=[vmem, vmem],
        out_shape=[
            jax.ShapeDtypeStruct((slots, rows), jnp.float32),
            jax.ShapeDtypeStruct((2 * blocks, width), jnp.float32),
        ],
        scratch_shapes=[
            pltpu.VMEM((2 * blocks, width, depth), jnp.bfloat16),
            pltpu.VMEM((slots, rows, depth), jnp.bfloat16),
            pltpu.VMEM((group * UNIT, depth), jnp.bfloat16),
            pltpu.VMEM((slots + 1, rows, width), jnp.float32),
            pltpu.VMEM((8 if turned else blocks, width, width), jnp.float32),
            pltpu.SMEM((2 * blocks,), jnp.int32),
            pltpu.SMEM((slots * 32,), jnp.int32),
            pltpu.SemaphoreType.DMA((3,)),
        ],
        compiler_params=pltpu.CompilerParams(vmem_limit_bytes=(24 if turned else 45 if places <= 8 else 56) * MIB),
        cost_estimate=pl.CostEstimate(
            flops=2 * slots * rows * width * depth, bytes_accessed=2 * slots * rows * depth, transcendentals=0
        ),
        name="score",
    )(codes.reshape(-1), counts, jnp.asarray(near_pairs(blocks).reshape(-1)), linked, near, far, arrived)


def one_hot(index, count, valid):
    return (index[:, None] == jnp.arange(count, dtype=jnp.int32)[None, :]) & valid[:, None]


def exchange(values, chips):
    groups = [[2 * x + c for x in range(chips)] for c in range(2)]
    return lax.all_to_all(values, "shard", split_axis=0, concat_axis=0, axis_index_groups=groups, tiled=True)


def far_maxima(direct, items, relayed, plan, counts, linked, near, far):
    send, own_far, codes, far_codes, hand, target, item_back, _ = plan
    blocks, width, depth = near.shape
    chips = send.shape[1]
    outgoing = pack(
        direct, items, send, own_far,
        near.reshape(-1, UNIT, depth), far.reshape(-1, UNIT, depth),
    )
    arrived = exchange(outgoing, chips)
    arrived, near, far, counts, linked, codes, far_codes, hand, target, item_back = lax.optimization_barrier(
        (arrived, near, far, counts, linked, codes, far_codes, hand, target, item_back)
    )
    if items:
        passed, target, item_back = relay(hand, arrived, target, item_back, direct, items)
        gained = exchange(passed, chips)
    back, best = score(codes, counts, linked, near, far, arrived, 16, False)
    places = direct
    if items:
        gained = gained.reshape(CLASSES, chips // CLASSES * relayed, depth)
        far_back, far_best = score(far_codes, counts, linked, near, far, gained, 4, True)
        best = jnp.maximum(best, far_best)
        hit = item_back.reshape(turns(direct), CLASSES, chips)[..., None] == jnp.arange(relayed, dtype=jnp.int32)
        far_back = far_back.reshape(1, CLASSES, 1, relayed, UNIT)
        far_back = jnp.where(hit[..., None], far_back, -1.0).max(axis=3)
        far_back = far_back.transpose(2, 0, 1, 3).reshape(chips, -1)
        back = jnp.concatenate([back, far_back], axis=1)
        places = direct + turns(direct) * CLASSES
    returned = exchange(back, chips)
    spots = target.T.reshape(-1)
    values = returned.reshape(-1, UNIT).T
    hit = spots[:, None] == jnp.arange(2 * blocks * width // UNIT, dtype=jnp.int32)[None, :]
    folded = jnp.where(hit[None], values[:, :, None], -1.0).max(axis=1)
    best = jnp.maximum(best, folded.T.reshape(2 * blocks, width))
    other = lax.ppermute(best[blocks:], "shard", [(d, d ^ 1) for d in range(2 * chips)])
    return jnp.maximum(best[:blocks], other)


def on_device(embeddings, block_rows, pairs):
    blocks = block_rows.shape[0]
    width = embeddings.shape[0] // blocks
    peers = lax.axis_size("shard")
    myself = lax.axis_index("shard")
    swap = [(d, d ^ 1) for d in range(peers)]
    row_block, col_block = pairs[:, 0], pairs[:, 1]
    alive = pairs[:, 2] == myself
    owner = row_block // blocks
    remote = alive & (owner != myself)
    row_local, col_local = row_block % blocks, col_block % blocks
    tell = ask(myself, pairs, block_rows, peers)
    told = lax.all_to_all(tell, "shard", split_axis=0, concat_axis=0, tiled=True)[:, 0]

    unit = normalize(embeddings, tell)
    near = unit.reshape(blocks, width, -1)
    far = lax.ppermute(near, "shard", swap)

    nearby = alive & ~remote
    row_table = one_hot(row_local, blocks, nearby).astype(jnp.float32)
    col_table = one_hot(col_local, blocks, nearby).astype(jnp.float32)
    adjacency = (
        lax.dot_general(row_table, col_table, (((0,), (0,)), ((), ())), preferred_element_type=jnp.float32) > 0.5
    )
    linked = (adjacency | adjacency.T).astype(jnp.int32).reshape(-1)

    plan = make_plan(*PLANS[0], told, myself)
    counts = jnp.concatenate([block_rows, lax.dynamic_slice_in_dim(told, myself ^ 1, 1, 0)[0, peers:]])

    def attempt(level, plan):
        def here():
            return far_maxima(*PLANS[level], plan, counts, linked, near, far)

        def later():
            return attempt(level + 1, make_plan(*PLANS[level + 1], told, myself))

        return lax.cond(plan[-1][0] > 0, here, later) if level + 1 < len(PLANS) else here()

    return attempt(0, plan)


def solution(mesh):
    placed = (P("shard", None), P("shard"), P("shard", None))
    return jax.shard_map(
        on_device, mesh=mesh, in_specs=placed, out_specs=P("shard", None), check_vma=False
    )
```

profile of v0, /device:TPU:1, one launch (start us, length us, event | category | flops | bytes accessed | tf_op | source)
XLA Modules:
  0.0 323.0 jit_solution(10748539734860494466)
XLA Ops:
  0.0 1.5 ask.1.after_ref
  1.5 11.5 %all-to-all-start.8 = ((s32[128,1,144]{2,1,0:T(1,128)}), s32[128,1,144]{2,1,0:T(1,128)S(1)}, u32[]{:S(2)}, u32[]{:S(2)}) async-start(s32[128,1,144]{2,1,0:T(1,128)} %ask.1.after_ref), calls=%async_computation.8 | async-start | bytes 262144 | tf_op jit(solution)/shard_map/all_to_all | solution.py:656
  13.0 4.3 %normalize.1 = bf16[2048,1024]{1,0:T(8,128)(2,1)} custom-call(s32[128,1,144]{2,1,0:T(1,128)} %ask.1.after_ref, bf16[2048,1024]{1,0:T(8,128)(2,1)} %values_ref.1), custom_call_target="tpu_custom_call" | custom-call | flops 8388608 | bytes 8388608 | tf_op jit(solution)/shard_map/normalize/pallas_call | solution.py:63
  17.3 1.1 collective-permute-start.3
  18.4 0.7 and_select_fusion
  19.1 0.8 and_reduce_fusion
  19.9 0.5 convolution_compare_fusion
  20.6 2.1 all-to-all-done.8
  23.1 6.4 %plan.5 = (s32[7,64]{1,0:T(8,128)S(1)}, s32[16,4]{1,0:T(8,128)S(1)}, s32[7,64]{1,0:T(8,128)S(1)}, s32[24,4]{1,0:T(8,128)S(1)}, s32[64,24]{1,0:T(8,128)S(1)}, /*i...) custom-call(s32[1]{0:T(128)} %bitcast.32.me_ref, s32[128,128]{1,0:T(8,128)S(1)} %copy.76.pair_ref, ...), custom_call_target="tpu_custom_call" | custom-call | flops 99999997952 | bytes 1000000 | tf_op jit(solution)/shard_map/plan/pallas_call | solution.py:332
  30.2 292.2 %conditional.2 = (f32[16,128]{1,0:T(8,128)S(1)}) conditional(s32[]{:T(128)} %bitcast.37, (s32[]{:T(128)}, s32[128,144]{0,1:T(8,128)S(1)}, bf16[2048,1024]{1,0:T(8,128)(2,1)}, bf16[16,128,1024]{2,1,0:T(8,128)(2,1)}, bf16[16,128,1024]{2,1,0:T(8,128)(2,1)}, /*index=5*/s32[32]{0:T(128)S(1)}, s32[256]{0:T(256)S(1)}, s32[40]{0:T(128)S(1)}, ...), branch_computations={%region_0.6_spmd, %region_6.9_spmd} | conditional | flops 204303597568 | bytes 104855184 | solution.py:680
  30.6 6.0 %pack.5 = bf16[64,128,1024]{2,1,0:T(8,128)(2,1)S(1)} custom-call(s32[448]{0:T(512)S(1)} %reshape.186.send, s32[64]{0:T(128)S(1)} %reshape.187.far, bf16[128,16,1024]{2,1,0:T(8,128)(2,1)} %bitcast.66, bf16[128,16,1024]{2,1,0:T(8,128)(2,1)} %bitcast.23.far_ref), custom_call_target="tpu_custom_call" | custom-call | tf_op jit(solution)/shard_map/cond/branch_1_fun/pack/pallas_call | solution.py:406
  36.6 192.6 %all_to_all.48.arrived_ref.held_ref = bf16[64,128,1024]{2,1,0:T(8,128)(2,1)} all-to-all(bf16[64,128,1024]{2,1,0:T(8,128)(2,1)S(1)} %pack.5), channel_id=1, replica_groups={{0,2,4,6,8,10,12,14,16,18,20,22,24,26,28,30,32,34,36,38,40,42,44,46,48,..., dimensions={0} | all-to-all | bytes 33554432 | tf_op jit(solution)/shard_map/cond/branch_1_fun/all_to_all | solution.py:604
  229.2 7.0 %relay.3 = (bf16[1536,1024]{1,0:T(8,128)(2,1)}, s32[19,64]{1,0:T(8,128)}, s32[12,64]{1,0:T(8,128)}) custom-call(s32[64,24]{1,0:T(8,128)S(1)} %get-tuple-element.195.hand_ref, bf16[64,128,1024]{2,1,0:T(8,128)(2,1)} %all_to_all.48.arrived_ref.held_ref, s32[19,64]{1,0:T(8,128)S(1)} %get-tuple-element.196.target_ref, s32[12,64]{1,0:T(8,128)S(1)} %get-tuple-element.197.back_ref), custom_call_target="tpu_custom_call" | custom-call | tf_op jit(solution)/shard_map/cond/branch_1_fun/relay/pallas_call | solution.py:451
  236.2 12.8 %all-to-all-start.6 = ((bf16[64,24,1024]{2,1,0:T(8,128)(2,1)}), bf16[64,24,1024]{2,1,0:T(8,128)(2,1)S(1)}, u32[]{:S(2)}, u32[]{:S(2)}) async-start(bf16[64,24,1024]{2,1,0:T(8,128)(2,1)} %bitcast.67), calls=%async_computation.6 | async-start | bytes 6291456 | tf_op jit(solution)/shard_map/cond/branch_1_fun/all_to_all | solution.py:604
  249.1 0.7 eq.121
  249.8 0.8 copy.70
  250.6 0.1 eq.117
  250.8 26.2 %score.8 = (f32[64,112]{1,0:T(8,128)S(1)}, f32[32,128]{1,0:T(8,128)S(1)}) custom-call(s32[448]{0:T(512)S(1)} %reshape.189.codes, s32[32]{0:T(128)S(1)} %get-tuple-element.186.counts, s32[40]{0:T(128)S(1)} %get-tuple-element.194.near, s32[256]{0:T(256)S(1)} %get-tuple-element.188.linked, bf16[16,128,1024]{2,1,0:T(8,128)(2,1)} %get-tuple-element.189.near_ref, ...), custom_call_target="tpu_custom_call" | custom-call | flops 1879048192 | bytes 14680064 | tf_op jit(solution)/shard_map/cond/branch_1_fun/score/pallas_call | solution.py:572
  277.1 9.9 %all-to-all-done.6 = bf16[64,24,1024]{2,1,0:T(8,128)(2,1)S(1)} async-done(((bf16[64,24,1024]{2,1,0:T(8,128)(2,1)}), bf16[64,24,1024]{2,1,0:T(8,128)(2,1)S(1)}, u32[]{:S(2)}, u32[]{:S(2)}) %all-to-all-start.6) | async-done | bytes 3145760 | tf_op jit(solution)/shard_map/cond/branch_1_fun/all_to_all | solution.py:604
  287.0 9.0 %score.9 = (f32[4,384]{1,0:T(4,128)S(1)}, f32[32,128]{1,0:T(8,128)S(1)}) custom-call(s32[96]{0:T(128)S(1)} %reshape.190.codes, s32[32]{0:T(128)S(1)} %get-tuple-element.186.counts, s32[40]{0:T(128)S(1)} %get-tuple-element.194.near, s32[256]{0:T(256)S(1)} %get-tuple-element.188.linked, bf16[16,128,1024]{2,1,0:T(8,128)(2,1)} %get-tuple-element.189.near_ref, ...), custom_call_target="tpu_custom_call" | custom-call | flops 402653184 | bytes 3145728 | tf_op jit(solution)/shard_map/cond/branch_1_fun/score/pallas_call | solution.py:572
  296.1 0.4 select_reduce_fusion.4
  296.5 0.7 copy.72
  297.3 9.1 %all-to-all-start.7 = ((f32[64,1,304]{2,1,0:T(1,128)}), f32[64,1,304]{2,1,0:T(1,128)S(1)}, u32[]{:S(2)}, u32[]{:S(2)}) async-start(f32[64,1,304]{2,1,0:T(1,128)} %copy.72), calls=%async_computation.7 | async-start | bytes 196608 | tf_op jit(solution)/shard_map/cond/branch_1_fun/all_to_all | solution.py:604
  306.5 0.2 iota_compare_fusion.3
  306.7 8.3 %all-to-all-done.7 = f32[64,1,304]{2,1,0:T(1,128)S(1)} async-done(((f32[64,1,304]{2,1,0:T(1,128)}), f32[64,1,304]{2,1,0:T(1,128)S(1)}, u32[]{:S(2)}, u32[]{:S(2)}) %all-to-all-start.7) | async-done | bytes 77856 | tf_op jit(solution)/shard_map/cond/branch_1_fun/all_to_all | solution.py:604
  315.0 0.2 reduce.2
  315.2 0.3 reshape.194
  315.5 0.2 copy.73
  315.6 3.2 select_reduce_fusion.3
  319.1 2.5 collective-permute-start.2
  321.6 0.8 collective-permute-done.2
  322.4 0.6 copy-done.1
  (31 shorter events, 1.3 us)
Async XLA Ops:
  1.5 21.2 %all-to-all-start.8 = ((s32[128,1,144]{2,1,0:T(1,128)}), s32[128,1,144]{2,1,0:T(1,128)S(1)}, u32[]{:S(2)}, u32[]{:S(2)}) async-start(s32[128,1,144]{2,1,0:T(1,128)} %ask.1.after_ref), calls=%async_computation.8 | async-start | bytes 262144 | tf_op jit(solution)/shard_map/all_to_all | solution.py:656
  17.3 12.9 %collective-permute-start.3 = (bf16[16,128,1024]{2,1,0:T(8,128)(2,1)}, bf16[16,128,1024]{2,1,0:T(8,128)(2,1)}, u32[]{:S(2)}, u32[]{:S(2)}) collective-permute-start(bf16[16,128,1024]{2,1,0:T(8,128)(2,1)} %bitcast.59), channel_id=1, source_target_pairs={{0,1},{1,0},{2,3},{3,2},{4,5},{5,4},{6,7},{7,6},{8,9},{9,8},{10,11... | collective-permute-start | bytes 12582920 | tf_op jit(solution)/shard_map/ppermute | solution.py:660
  23.1 7.1 %copy-start.3 = (s32[16]{0:T(128)S(1)}, s32[16]{0:T(128)}, u32[]{:S(2)}) copy-start(s32[16]{0:T(128)} %param.13) | copy-start | bytes 196
  23.1 7.2 %copy-start = (s32[40]{0:T(128)S(1)}, s32[40]{0:T(128)}, u32[]{:S(2)}) copy-start(s32[40]{0:T(128)} %constant.63.clone) | copy-start | bytes 484
  236.2 50.8 %all-to-all-start.6 = ((bf16[64,24,1024]{2,1,0:T(8,128)(2,1)}), bf16[64,24,1024]{2,1,0:T(8,128)(2,1)S(1)}, u32[]{:S(2)}, u32[]{:S(2)}) async-start(bf16[64,24,1024]{2,1,0:T(8,128)(2,1)} %bitcast.67), calls=%async_computation.6 | async-start | bytes 6291456 | tf_op jit(solution)/shard_map/cond/branch_1_fun/all_to_all | solution.py:604
  297.3 17.7 %all-to-all-start.7 = ((f32[64,1,304]{2,1,0:T(1,128)}), f32[64,1,304]{2,1,0:T(1,128)S(1)}, u32[]{:S(2)}, u32[]{:S(2)}) async-start(f32[64,1,304]{2,1,0:T(1,128)} %copy.72), calls=%async_computation.7 | async-start | bytes 196608 | tf_op jit(solution)/shard_map/cond/branch_1_fun/all_to_all | solution.py:604
  319.1 3.4 %collective-permute-start.2 = (f32[16,128]{1,0:T(8,128)S(1)}, f32[16,128]{1,0:T(8,128)S(1)}, u32[]{:S(2)}, u32[]{:S(2)}) collective-permute-start(f32[16,128]{1,0:T(8,128)S(1)} %slice.64), channel_id=1, source_target_pairs={{0,1},{1,0},{2,3},{3,2},{4,5},{5,4},{6,7},{7,6},{8,9},{9,8},{10,11... | collective-permute-start | bytes 24584 | tf_op jit(solution)/shard_map/cond/branch_1_fun/ppermute | solution.py:640
  322.4 0.6 copy-start.1
where the time goes:
time: 323 us
  blocking collectives  193 us (60%)
  Pallas kernels  60.3 us (19%)
  starting transfers between devices  37 us (11%)
  waiting for transfers between devices  21.1 us (7%)
  other arithmetic  5.75 us (2%)
  local copies, waits for them, and re-layouts  4.62 us (1%)
    all_to_all x1, blocking collectives, exchange(): lax.all_to_all(values, 'shard', split_axis=0, concat_axis=0, axis_index_g...  193 us
    pallas_call x2, Pallas kernels, score(): pl.pallas_call(functools.partial(score_kernel, places, group, turned), in...  35.2 us
    all_to_all x2, starting transfers between devices, exchange(): lax.all_to_all(values, 'shard', split_axis=0, concat_axis=0, axis_index_g...  21.9 us
    all_to_all x2, waiting for transfers between devices, exchange(): lax.all_to_all(values, 'shard', split_axis=0, concat_axis=0, axis_index_g...  18.1 us
    all_to_all x1, starting transfers between devices, on_device(): lax.all_to_all(tell, 'shard', split_axis=0, concat_axis=0, tiled=True)[:, 0]  11.5 us
    pallas_call x1, Pallas kernels, relay(): pl.pallas_call(relay_kernel, grid=(chips * relayed // step,), in_specs=[p...  6.96 us
  transfers between devices with their start and end apart: 5, of which 4 were waited for; matrix products, arithmetic and copies ran while one was open for 1% of the time, Pallas kernels for 11%

commit v1 on v0

--- a/solution.py
+++ b/solution.py
@@ -355,11 +355,14 @@
     )(device.reshape(1), told[:, :devices], told[:, devices:], told[:, devices:].T)
 
 
-def turn(first, second, values):
+def turning(first, second):
     rows = first * second
     o = lax.broadcasted_iota(jnp.int32, (rows, rows), 0)
     i = lax.broadcasted_iota(jnp.int32, (rows, rows), 1)
-    take = ((o % first) * second + o // first == i).astype(jnp.float32).astype(jnp.bfloat16)
+    return ((o % first) * second + o // first == i).astype(jnp.float32).astype(jnp.bfloat16)
+
+
+def turn(take, values):
     return jnp.dot(take, values, preferred_element_type=jnp.float32).astype(jnp.bfloat16)
 
 
@@ -383,11 +386,12 @@
     def _():
         fetch(near_ref, far_ref, held, sems)
         if items:
+            take = turning(items, UNIT)
             for p in range(CLASSES):
                 for q in range(items):
                     gathered[pl.ds(q * UNIT, UNIT), :] = held[far[q * CLASSES + p]]
                 size = items * UNIT
-                turned[pl.ds(p * size, size), :] = turn(items, UNIT, gathered[...])
+                turned[pl.ds(p * size, size), :] = turn(take, gathered[...])
 
     for k in range(group):
         slot = step * group + k
@@ -507,10 +511,12 @@
         return carry
 
     lax.fori_loop(0, slots, link, 0)
+    if turned:
+        take = turning(UNIT, places)
     copies[0].wait()
     if turned:
         for slot in range(slots):
-            rows_held[slot] = turn(UNIT, places, rows_held[slot])
+            rows_held[slot] = turn(take, rows_held[slot])
     else:
         score_near(near, linked, counts, held, best_ref, kept)
     for copy in copies[1:]:

time: 323 us -> 324 us (level)
  no operation moved by 1% of the time
where the time goes in v1:
time: 324 us; the launch traced here: 323 us
  blocking collectives  193 us (60%)
  Pallas kernels  60.2 us (19%)
  starting transfers between devices  37 us (11%)
  waiting for transfers between devices  21.4 us (7%)
  other arithmetic  5.75 us (2%)
  local copies, waits for them, and re-layouts  4.62 us (1%)
    all_to_all x1, blocking collectives, exchange(): lax.all_to_all(values, 'shard', split_axis=0, concat_axis=0, axis_index_g...  193 us
    pallas_call x2, Pallas kernels, score(): pl.pallas_call(functools.partial(score_kernel, places, group, turned), in...  35.1 us
    all_to_all x2, starting transfers between devices, exchange(): lax.all_to_all(values, 'shard', split_axis=0, concat_axis=0, axis_index_g...  21.4 us
    all_to_all x2, waiting for transfers between devices, exchange(): lax.all_to_all(values, 'shard', split_axis=0, concat_axis=0, axis_index_g...  18.5 us
    all_to_all x1, starting transfers between devices, on_device(): lax.all_to_all(tell, 'shard', split_axis=0, concat_axis=0, tiled=True)[:, 0]  11.5 us
    pallas_call x1, Pallas kernels, relay(): pl.pallas_call(relay_kernel, grid=(chips * relayed // step,), in_specs=[p...  6.96 us
  transfers between devices with their start and end apart: 5, of which 4 were waited for; matrix products, arithmetic and copies ran while one was open for 1% of the time, Pallas kernels for 11%

profile of v1, /device:TPU:1, one launch (start us, length us, event | category | flops | bytes accessed | tf_op | source)
XLA Modules:
  0.0 323.3 jit_solution(6952470757467519957)
XLA Ops:
  0.0 1.5 ask.1.after_ref
  1.5 11.5 %all-to-all-start.8 = ((s32[128,1,144]{2,1,0:T(1,128)}), s32[128,1,144]{2,1,0:T(1,128)S(1)}, u32[]{:S(2)}, u32[]{:S(2)}) async-start(s32[128,1,144]{2,1,0:T(1,128)} %ask.1.after_ref), calls=%async_computation.8 | async-start | bytes 262144 | tf_op jit(solution)/shard_map/all_to_all | solution.py:662
  13.0 4.3 %normalize.1 = bf16[2048,1024]{1,0:T(8,128)(2,1)} custom-call(s32[128,1,144]{2,1,0:T(1,128)} %ask.1.after_ref, bf16[2048,1024]{1,0:T(8,128)(2,1)} %values_ref.1), custom_call_target="tpu_custom_call" | custom-call | flops 8388608 | bytes 8388608 | tf_op jit(solution)/shard_map/normalize/pallas_call | solution.py:63
  17.3 1.1 collective-permute-start.3
  18.4 0.7 and_select_fusion
  19.1 0.8 and_reduce_fusion
  19.9 0.5 convolution_compare_fusion
  20.6 2.1 all-to-all-done.8
  23.1 6.4 %plan.5 = (s32[7,64]{1,0:T(8,128)S(1)}, s32[16,4]{1,0:T(8,128)S(1)}, s32[7,64]{1,0:T(8,128)S(1)}, s32[24,4]{1,0:T(8,128)S(1)}, s32[64,24]{1,0:T(8,128)S(1)}, /*i...) custom-call(s32[1]{0:T(128)} %bitcast.32.me_ref, s32[128,128]{1,0:T(8,128)S(1)} %copy.76.pair_ref, ...), custom_call_target="tpu_custom_call" | custom-call | flops 99999997952 | bytes 1000000 | tf_op jit(solution)/shard_map/plan/pallas_call | solution.py:332
  30.2 292.4 %conditional.2 = (f32[16,128]{1,0:T(8,128)S(1)}) conditional(s32[]{:T(128)} %bitcast.37, (s32[]{:T(128)}, s32[128,144]{0,1:T(8,128)S(1)}, bf16[2048,1024]{1,0:T(8,128)(2,1)}, bf16[16,128,1024]{2,1,0:T(8,128)(2,1)}, bf16[16,128,1024]{2,1,0:T(8,128)(2,1)}, /*index=5*/s32[32]{0:T(128)S(1)}, s32[256]{0:T(256)S(1)}, s32[40]{0:T(128)S(1)}, ...), branch_computations={%region_0.6_spmd, %region_6.9_spmd} | conditional | flops 204303597568 | bytes 104855184 | solution.py:686
  30.6 6.0 %pack.5 = bf16[64,128,1024]{2,1,0:T(8,128)(2,1)S(1)} custom-call(s32[448]{0:T(512)S(1)} %reshape.186.send, s32[64]{0:T(128)S(1)} %reshape.187.far, bf16[128,16,1024]{2,1,0:T(8,128)(2,1)} %bitcast.66, bf16[128,16,1024]{2,1,0:T(8,128)(2,1)} %bitcast.23.far_ref), custom_call_target="tpu_custom_call" | custom-call | tf_op jit(solution)/shard_map/cond/branch_1_fun/pack/pallas_call | solution.py:410
  36.6 192.6 %all_to_all.48.arrived_ref.held_ref = bf16[64,128,1024]{2,1,0:T(8,128)(2,1)} all-to-all(bf16[64,128,1024]{2,1,0:T(8,128)(2,1)S(1)} %pack.5), channel_id=1, replica_groups={{0,2,4,6,8,10,12,14,16,18,20,22,24,26,28,30,32,34,36,38,40,42,44,46,48,..., dimensions={0} | all-to-all | bytes 33554432 | tf_op jit(solution)/shard_map/cond/branch_1_fun/all_to_all | solution.py:610
  229.2 7.0 %relay.3 = (bf16[1536,1024]{1,0:T(8,128)(2,1)}, s32[19,64]{1,0:T(8,128)}, s32[12,64]{1,0:T(8,128)}) custom-call(s32[64,24]{1,0:T(8,128)S(1)} %get-tuple-element.195.hand_ref, bf16[64,128,1024]{2,1,0:T(8,128)(2,1)} %all_to_all.48.arrived_ref.held_ref, s32[19,64]{1,0:T(8,128)S(1)} %get-tuple-element.196.target_ref, s32[12,64]{1,0:T(8,128)S(1)} %get-tuple-element.197.back_ref), custom_call_target="tpu_custom_call" | custom-call | tf_op jit(solution)/shard_map/cond/branch_1_fun/relay/pallas_call | solution.py:455
  236.2 12.8 %all-to-all-start.6 = ((bf16[64,24,1024]{2,1,0:T(8,128)(2,1)}), bf16[64,24,1024]{2,1,0:T(8,128)(2,1)S(1)}, u32[]{:S(2)}, u32[]{:S(2)}) async-start(bf16[64,24,1024]{2,1,0:T(8,128)(2,1)} %bitcast.67), calls=%async_computation.6 | async-start | bytes 6291456 | tf_op jit(solution)/shard_map/cond/branch_1_fun/all_to_all | solution.py:610
  249.1 0.7 eq.121
  249.8 0.8 copy.70
  250.6 0.1 eq.117
  250.8 25.9 %score.8 = (f32[64,112]{1,0:T(8,128)S(1)}, f32[32,128]{1,0:T(8,128)S(1)}) custom-call(s32[448]{0:T(512)S(1)} %reshape.189.codes, s32[32]{0:T(128)S(1)} %get-tuple-element.186.counts, s32[40]{0:T(128)S(1)} %get-tuple-element.194.near, s32[256]{0:T(256)S(1)} %get-tuple-element.188.linked, bf16[16,128,1024]{2,1,0:T(8,128)(2,1)} %get-tuple-element.189.near_ref, ...), custom_call_target="tpu_custom_call" | custom-call | flops 1879048192 | bytes 14680064 | tf_op jit(solution)/shard_map/cond/branch_1_fun/score/pallas_call | solution.py:578
  276.8 10.2 %all-to-all-done.6 = bf16[64,24,1024]{2,1,0:T(8,128)(2,1)S(1)} async-done(((bf16[64,24,1024]{2,1,0:T(8,128)(2,1)}), bf16[64,24,1024]{2,1,0:T(8,128)(2,1)S(1)}, u32[]{:S(2)}, u32[]{:S(2)}) %all-to-all-start.6) | async-done | bytes 3145760 | tf_op jit(solution)/shard_map/cond/branch_1_fun/all_to_all | solution.py:610
  287.0 9.2 %score.9 = (f32[4,384]{1,0:T(4,128)S(1)}, f32[32,128]{1,0:T(8,128)S(1)}) custom-call(s32[96]{0:T(128)S(1)} %reshape.190.codes, s32[32]{0:T(128)S(1)} %get-tuple-element.186.counts, s32[40]{0:T(128)S(1)} %get-tuple-element.194.near, s32[256]{0:T(256)S(1)} %get-tuple-element.188.linked, bf16[16,128,1024]{2,1,0:T(8,128)(2,1)} %get-tuple-element.189.near_ref, ...), custom_call_target="tpu_custom_call" | custom-call | flops 402653184 | bytes 3145728 | tf_op jit(solution)/shard_map/cond/branch_1_fun/score/pallas_call | solution.py:578
  296.3 0.4 select_reduce_fusion.4
  296.8 0.7 copy.72
  297.5 8.6 %all-to-all-start.7 = ((f32[64,1,304]{2,1,0:T(1,128)}), f32[64,1,304]{2,1,0:T(1,128)S(1)}, u32[]{:S(2)}, u32[]{:S(2)}) async-start(f32[64,1,304]{2,1,0:T(1,128)} %copy.72), calls=%async_computation.7 | async-start | bytes 196608 | tf_op jit(solution)/shard_map/cond/branch_1_fun/all_to_all | solution.py:610
  306.1 0.2 iota_compare_fusion.3
  306.4 8.3 %all-to-all-done.7 = f32[64,1,304]{2,1,0:T(1,128)S(1)} async-done(((f32[64,1,304]{2,1,0:T(1,128)}), f32[64,1,304]{2,1,0:T(1,128)S(1)}, u32[]{:S(2)}, u32[]{:S(2)}) %all-to-all-start.7) | async-done | bytes 77856 | tf_op jit(solution)/shard_map/cond/branch_1_fun/all_to_all | solution.py:610
  314.6 0.2 reduce.2
  314.9 0.3 reshape.194
  315.1 0.2 copy.73
  315.3 3.2 select_reduce_fusion.3
  318.8 3.1 collective-permute-start.2
  321.8 0.8 collective-permute-done.2
  322.7 0.6 copy-done.1
  (31 shorter events, 1.3 us)
Async XLA Ops:
  1.5 21.2 %all-to-all-start.8 = ((s32[128,1,144]{2,1,0:T(1,128)}), s32[128,1,144]{2,1,0:T(1,128)S(1)}, u32[]{:S(2)}, u32[]{:S(2)}) async-start(s32[128,1,144]{2,1,0:T(1,128)} %ask.1.after_ref), calls=%async_computation.8 | async-start | bytes 262144 | tf_op jit(solution)/shard_map/all_to_all | solution.py:662
  17.3 12.9 %collective-permute-start.3 = (bf16[16,128,1024]{2,1,0:T(8,128)(2,1)}, bf16[16,128,1024]{2,1,0:T(8,128)(2,1)}, u32[]{:S(2)}, u32[]{:S(2)}) collective-permute-start(bf16[16,128,1024]{2,1,0:T(8,128)(2,1)} %bitcast.59), channel_id=1, source_target_pairs={{0,1},{1,0},{2,3},{3,2},{4,5},{5,4},{6,7},{7,6},{8,9},{9,8},{10,11... | collective-permute-start | bytes 12582920 | tf_op jit(solution)/shard_map/ppermute | solution.py:666
  23.1 7.1 %copy-start.3 = (s32[16]{0:T(128)S(1)}, s32[16]{0:T(128)}, u32[]{:S(2)}) copy-start(s32[16]{0:T(128)} %param.13) | copy-start | bytes 196
  23.1 7.2 %copy-start = (s32[40]{0:T(128)S(1)}, s32[40]{0:T(128)}, u32[]{:S(2)}) copy-start(s32[40]{0:T(128)} %constant.63.clone) | copy-start | bytes 484
  236.2 50.8 %all-to-all-start.6 = ((bf16[64,24,1024]{2,1,0:T(8,128)(2,1)}), bf16[64,24,1024]{2,1,0:T(8,128)(2,1)S(1)}, u32[]{:S(2)}, u32[]{:S(2)}) async-start(bf16[64,24,1024]{2,1,0:T(8,128)(2,1)} %bitcast.67), calls=%async_computation.6 | async-start | bytes 6291456 | tf_op jit(solution)/shard_map/cond/branch_1_fun/all_to_all | solution.py:610
  297.5 17.1 %all-to-all-start.7 = ((f32[64,1,304]{2,1,0:T(1,128)}), f32[64,1,304]{2,1,0:T(1,128)S(1)}, u32[]{:S(2)}, u32[]{:S(2)}) async-start(f32[64,1,304]{2,1,0:T(1,128)} %copy.72), calls=%async_computation.7 | async-start | bytes 196608 | tf_op jit(solution)/shard_map/cond/branch_1_fun/all_to_all | solution.py:610
  318.8 3.9 %collective-permute-start.2 = (f32[16,128]{1,0:T(8,128)S(1)}, f32[16,128]{1,0:T(8,128)S(1)}, u32[]{:S(2)}, u32[]{:S(2)}) collective-permute-start(f32[16,128]{1,0:T(8,128)S(1)} %slice.64), channel_id=1, source_target_pairs={{0,1},{1,0},{2,3},{3,2},{4,5},{5,4},{6,7},{7,6},{8,9},{9,8},{10,11... | collective-permute-start | bytes 24584 | tf_op jit(solution)/shard_map/cond/branch_1_fun/ppermute | solution.py:646
  322.7 0.6 copy-start.1
